TPU v7x, 128 devices: a whole 4x4x4 slice. The times are simulated.
128 devices in a mesh: tile: 16 (over z, y), seq: 8 (over x, core).
Axes of the slice: x: 4, y: 4, z: 4, core: 2. Of those that a mesh axis runs over, the one named last changes fastest.
Arguments:
- cls_tokens: bfloat16 [16384, 1536], P(('tile', 'seq')), may hold values from -6 to 6
- norm_gain: float32 [1536], replicated, may hold values from 0.5 to 1.5
- w_gate: bfloat16 [1536, 4096], P(None, 'tile'), may hold values from -0.15625 to 0.15625
- w_up: bfloat16 [1536, 4096], P(None, 'tile'), may hold values from -0.15625 to 0.15625
- w_down: bfloat16 [4096, 1536], P('tile'), may hold values from -0.09375 to 0.09375
- layer_scale: float32 [1536], replicated, may hold values from 0.25 to 1.75
- final_gain: float32 [1536], replicated, may hold values from 0.5 to 1.5
- w_embed: bfloat16 [1536, 768], replicated, may hold values from -0.15625 to 0.15625
- dest_pos: int32 [16384], P(('tile', 'seq')), may hold values from 0 to 16383, as said below
- tile_coords: int32 [2, 16384], P(None, ('tile', 'seq')), may hold values from 0 to 999
- attn_gain: float32 [768], replicated, may hold values from 0.5 to 1.5
- w_qkv: bfloat16 [768, 2304], replicated, may hold values from -4 to 4
- offsets: int32 [12], replicated, may hold values from 0 to 15
- w_out: bfloat16 [768, 768], replicated, may hold values from -0.21875 to 0.21875
Outputs:
- slide_out: bfloat16 [16384, 768], P(('tile', 'seq'))
Inputs may be any that keep to these rules, and one draw needn't show every extreme that they name: dest_pos holds each number of 0 to 16383 once; the 128 rows of one device go to the devices of the slide order in groups of 0, 1 or 2 rows a device, some pair carrying 2; every device receives 128 rows, 2 of them from the device 128 / 2 places before it in the slide order, counted round.
All inputs are finite; a program needn't handle non-finite values.
Results may differ from a plain program's by a relative error of at most 0.018.
Values may be sent and summed in bfloat16 or wider, within the bound.
No kernel may reach another device: no remote copies, remote signals or barrier semaphores. Data moves between devices by JAX's collectives and lax.ppermute only.
A program may use at most 128 MiB of HBM per device.

v0:
```python
import jax
import jax.numpy as jnp
from jax import lax
from jax.sharding import PartitionSpec as P

HEAD_COUNT = 12
HEAD_WIDTH = 64
SEGMENT_SPACING = 16


def layer_norm(sender_rows, gain):
    average = jnp.mean(sender_rows, axis=-1, keepdims=True)
    centered = sender_rows - average
    variance = jnp.mean(centered * centered, axis=-1, keepdims=True)
    return centered * lax.rsqrt(variance + 1e-06) * gain


def position_table(coords, hidden_width):
    quarter = hidden_width // 4
    frequency = 1.0 / 10000.0 ** (jnp.arange(quarter).astype(jnp.float32) / quarter)
    along_x = coords[:, 0:1].astype(jnp.float32) * frequency[None, :]
    along_y = coords[:, 1:2].astype(jnp.float32) * frequency[None, :]
    return jnp.concatenate(
        [jnp.sin(along_x), jnp.cos(along_x), jnp.sin(along_y), jnp.cos(along_y)], axis=1
    )


def attend(queries, key_rows, values):
    score_scale = queries.shape[-1] ** (-0.5)
    scores = (
        jnp.einsum("qhd,khd->hqk", queries, key_rows, preferred_element_type=jnp.float32)
        * score_scale
    )
    highest = jnp.max(scores, axis=-1, keepdims=True)
    weights = jnp.exp(scores - highest)
    totals = jnp.sum(weights, axis=-1, keepdims=True)
    mixed_rows = jnp.einsum(
        "hqk,khd->qhd", weights.astype(jnp.bfloat16), values, preferred_element_type=jnp.float32
    )
    result = mixed_rows / jnp.transpose(totals, (1, 0, 2))
    logsum = jnp.transpose((highest + jnp.log(totals))[:, :, 0])
    return (result, logsum)


def body(
    cls_tokens,
    norm_gain,
    w_gate,
    w_up,
    w_down,
    layer_scale,
    final_gain,
    w_embed,
    dest_pos,
    tile_coords,
    attn_gain,
    w_qkv,
    offsets,
    w_out,
):
    resident_rows = cls_tokens.shape[0]
    tokens = cls_tokens.astype(jnp.float32)
    normed = layer_norm(tokens, norm_gain).astype(jnp.bfloat16)
    shard_rows = lax.all_gather(normed, "tile", axis=0, tiled=True)
    gate_proj = jnp.dot(shard_rows, w_gate, preferred_element_type=jnp.float32)
    upward = jnp.dot(shard_rows, w_up, preferred_element_type=jnp.float32)
    hidden = (jax.nn.silu(gate_proj) * upward).astype(jnp.bfloat16)
    projected = lax.psum_scatter(
        jnp.dot(hidden, w_down, preferred_element_type=jnp.float32),
        "tile",
        scatter_dimension=0,
        tiled=True,
    )
    mixed_rows = tokens + layer_scale * projected
    final_rows = layer_norm(mixed_rows, final_gain).astype(jnp.bfloat16)
    embedded = jnp.dot(final_rows, w_embed, preferred_element_type=jnp.float32).astype(jnp.bfloat16)
    hidden_width = embedded.shape[1]
    tile_count = lax.axis_size("tile")
    seq_count = lax.axis_size("seq")
    devices = tile_count * seq_count
    capacity = 2 * max(1, resident_rows // devices)
    target = dest_pos // resident_rows
    row_ids = jnp.arange(resident_rows)
    earlier = (target[:, None] == target[None, :]) & (row_ids[None, :] < row_ids[:, None])
    slot_index = jnp.sum(earlier.astype(jnp.int32), axis=1)
    where_to = target * capacity + slot_index
    payload = jnp.zeros((devices * capacity, hidden_width), jnp.bfloat16).at[where_to].set(embedded)
    meta_rows = jnp.stack([dest_pos, tile_coords[0], tile_coords[1]], axis=1)
    meta_table = jnp.full((devices * capacity, 3), -1, jnp.int32).at[where_to].set(meta_rows)
    received, received_meta = (
        lax.all_to_all(
            payload.reshape(devices, capacity, hidden_width),
            ("tile", "seq"),
            split_axis=0,
            concat_axis=0,
            tiled=True,
        ),
        lax.all_to_all(
            meta_table.reshape(devices, capacity, 3),
            ("tile", "seq"),
            split_axis=0,
            concat_axis=0,
            tiled=True,
        ),
    )
    flat_rows = received.reshape(-1, hidden_width)
    flat_meta = received_meta.reshape(-1, 3)
    is_live = flat_meta[:, 0] >= 0
    local_slot = jnp.where(is_live, flat_meta[:, 0] % resident_rows, resident_rows)
    placed = (
        jnp.zeros((resident_rows, hidden_width), jnp.bfloat16)
        .at[local_slot]
        .set(flat_rows, mode="drop")
    )
    coords = (
        jnp.zeros((resident_rows, 2), jnp.int32).at[local_slot].set(flat_meta[:, 1:], mode="drop")
    )
    seq_in = placed.astype(jnp.float32) + position_table(coords, hidden_width)
    normed_seq = layer_norm(seq_in, attn_gain).astype(jnp.bfloat16)
    qkv = jnp.dot(normed_seq, w_qkv, preferred_element_type=jnp.float32).astype(jnp.bfloat16)
    queries = qkv[:, :hidden_width]
    keys_values = qkv[:, hidden_width:]
    segment_kv = lax.all_gather(keys_values, "seq", axis=0, tiled=True)
    near_out, nearby_logsumexp = attend(
        queries.reshape(resident_rows, HEAD_COUNT, HEAD_WIDTH),
        segment_kv[:, :hidden_width].reshape(-1, HEAD_COUNT, HEAD_WIDTH),
        segment_kv[:, hidden_width:].reshape(-1, HEAD_COUNT, HEAD_WIDTH),
    )
    kept_rows = jnp.arange(SEGMENT_SPACING, dtype=jnp.int32)[:, None] == offsets[None, :]

    def select(sender_rows, stacked_rows):
        head_grouped = sender_rows.reshape(
            resident_rows // SEGMENT_SPACING, SEGMENT_SPACING, stacked_rows, HEAD_COUNT, HEAD_WIDTH
        )
        sampled_rows = jnp.sum(
            jnp.where(
                kept_rows[None, :, None, :, None], head_grouped, jnp.zeros((), sender_rows.dtype)
            ),
            axis=1,
        )
        return sampled_rows.reshape(resident_rows // SEGMENT_SPACING, stacked_rows * hidden_width)

    far_kv = lax.all_gather(select(keys_values, 2), ("tile", "seq"), axis=0, tiled=True)
    far_out, far_lse = attend(
        select(queries, 1).reshape(-1, HEAD_COUNT, HEAD_WIDTH),
        far_kv[:, :hidden_width].reshape(-1, HEAD_COUNT, HEAD_WIDTH),
        far_kv[:, hidden_width:].reshape(-1, HEAD_COUNT, HEAD_WIDTH),
    )
    far_full = jnp.where(kept_rows[None, :, :, None], far_out[:, None], 0.0).reshape(
        resident_rows, HEAD_COUNT, HEAD_WIDTH
    )
    nearby_grouped = nearby_logsumexp.reshape(
        resident_rows // SEGMENT_SPACING, SEGMENT_SPACING, HEAD_COUNT
    )
    far_share = jnp.where(
        kept_rows[None], 1.0 / (1.0 + jnp.exp(nearby_grouped - far_lse[:, None])), 0.0
    ).reshape(resident_rows, HEAD_COUNT)
    combined = (1.0 - far_share)[:, :, None] * near_out + far_share[:, :, None] * far_full
    attn_rows = combined.reshape(resident_rows, hidden_width).astype(jnp.bfloat16)
    return (seq_in + jnp.dot(attn_rows, w_out, preferred_element_type=jnp.float32)).astype(
        jnp.bfloat16
    )


def solution(mesh):
    in_specs = (
        P(("tile", "seq"), None),
        P(),
        P(None, "tile"),
        P(None, "tile"),
        P("tile", None),
        P(),
        P(),
        P(),
        P(("tile", "seq")),
        P(None, ("tile", "seq")),
        P(),
        P(),
        P(),
        P(),
    )
    out_specs = P(("tile", "seq"), None)
    return jax.shard_map(body, mesh=mesh, in_specs=in_specs, out_specs=out_specs, check_vma=False)
```

profile of v0, /device:TPU:1, one launch (start us, length us, event | category | flops | bytes accessed | tf_op | source)
XLA Modules:
  0.0 357.2 jit_solution(11485548192163310712)
XLA Ops:
  6.5 1.3 convert_reduce_fusion
  7.8 1.2 fusion.31
  9.1 2.0 fusion.33
  11.2 64.7 %all-gather.4.cloned.1.call-done = bf16[2048,1536]{1,0:T(8,128)(2,1)} async-done(((bf16[128,1536]{1,0:T(8,128)(2,1)}), bf16[2048,1536]{1,0:T(8,128)(2,1)}) %all-gather.4.cloned.1.call-update) | async-done | bytes 6291472 | tf_op jit(solution)/shard_map/all_gather | solution.py:64
  75.9 6.1 %fusion.70 = f32[2048,256]{1,0:T(8,128)} fusion(bf16[2048,1536]{1,0:T(8,128)(2,1)} %all-gather.4.cloned.1.call-done, bf16[1536,256]{1,0:T(8,128)(2,1)} %param.16), kind=kOutput, calls=%fused_computation.112 | convolution fusion | flops 1610612736 | bytes 9175040 | tf_op jit(solution)/shard_map/dot_general | solution.py:65
  82.0 14.6 %fusion.7 = f32[2048,1536]{1,0:T(8,128)} fusion(bf16[256,1536]{1,0:T(8,128)(2,1)} %param.18, bf16[2048,1536]{1,0:T(8,128)(2,1)} %all-gather.4.cloned.1.call-done, bf16[1536,256]{1,0:T(8,128)(2,1)} %param.17, f32[2048,256]{1,0:T(8,128)} %fusion.70), kind=kOutput, calls=%fused_computation.14 | convolution fusion | flops 3224371200 | bytes 22544384 | tf_op jit(solution)/shard_map/dot_general | solution.py:69
  96.6 0.8 slice_bitcast_fusion.1
  97.4 1.2 pad_add_fusion
  98.6 1.4 copy.75
  100.0 0.7 and_select_fusion.1
  100.9 1.2 compare_select_fusion.4
  102.0 1.8 scatter_custom_fusion
  103.8 8.3 %all-to-all-start = ((s32[128,2,3]{2,1,0:T(2,128)}), s32[128,2,3]{2,1,0:T(2,128)}, u32[]{:S(2)}, u32[]{:S(2)}) async-start(s32[128,2,3]{2,1,0:T(2,128)} %bitcast.76), calls=%async_computation | async-start | bytes 262144 | tf_op jit(solution)/shard_map/all_to_all | solution.py:98
  112.8 9.2 %all-to-all-done = s32[128,2,3]{2,1,0:T(2,128)} async-done(((s32[128,2,3]{2,1,0:T(2,128)}), s32[128,2,3]{2,1,0:T(2,128)}, u32[]{:S(2)}, u32[]{:S(2)}) %all-to-all-start) | async-done | bytes 3104 | tf_op jit(solution)/shard_map/all_to_all | solution.py:98
  122.0 1.5 copy.93
  123.5 68.9 %reduce-scatter.2.cloned.1.call-done = f32[128,1536]{1,0:T(8,128)} async-done(((f32[2048,1536]{1,0:T(8,128)}), f32[128,1536]{1,0:T(8,128)}) %reduce-scatter.2.cloned.1.call-update) | async-done | bytes 786448 | tf_op jit(solution)/shard_map/reduce_scatter | solution.py:68
  192.4 1.5 fusion.39
  193.9 1.5 multiply_reduce_fusion.1
  195.4 2.9 convolution_convert_fusion.1
  198.3 2.3 scatter_custom_fusion.1
  200.6 1.9 reshape.194
  202.5 7.8 %all-to-all-start.1 = ((bf16[128,2,768]{2,1,0:T(2,128)(2,1)}), bf16[128,2,768]{2,1,0:T(2,128)(2,1)}, u32[]{:S(2)}, u32[]{:S(2)}) async-start(bf16[128,2,768]{2,1,0:T(2,128)(2,1)} %reshape.194), calls=%async_computation.2 | async-start | bytes 786432 | tf_op jit(solution)/shard_map/all_to_all | solution.py:91
  210.3 0.6 compare_select_fusion
  211.0 2.2 scatter_custom_fusion.3
  213.2 1.1 fusion.52
  214.3 2.5 multiply_sine_fusion.1
  216.7 5.6 %all-to-all-done.1 = bf16[128,2,768]{2,1,0:T(2,128)(2,1)} async-done(((bf16[128,2,768]{2,1,0:T(2,128)(2,1)}), bf16[128,2,768]{2,1,0:T(2,128)(2,1)}, u32[]{:S(2)}, u32[]{:S(2)}) %all-to-all-start.1) | async-done | bytes 393248 | tf_op jit(solution)/shard_map/all_to_all | solution.py:91
  222.3 1.9 reshape.224
  224.2 2.7 scatter_custom_fusion.2
  226.9 1.4 fusion.66
  228.6 0.7 convolution_convert_fusion
  229.3 0.8 copy-done.7
  230.1 0.8 slice.54
  231.0 2.6 reshape.199
  233.5 2.2 select_reduce_fusion
  235.8 1.6 reshape.200
  237.4 0.7 copy.80
  238.1 0.7 broadcast_in_dim.118
  238.7 0.7 broadcast_in_dim.119
  239.4 1.6 slice.53
  241.1 1.8 copy.81
  242.8 2.1 reshape.198
  244.9 1.9 select_reduce_fusion.1
  246.8 8.7 %all-gather.6.cloned.1.call-done = bf16[1024,1536]{1,0:T(8,128)(2,1)} async-done(((bf16[128,1536]{1,0:T(8,128)(2,1)}), bf16[1024,1536]{1,0:T(8,128)(2,1)}) %all-gather.6.cloned.1.call-update) | async-done | bytes 3145744 | tf_op jit(solution)/shard_map/all_gather | solution.py:123
  255.4 3.8 %fusion.68 = (bf16[1024,768]{1,0:T(8,128)(2,1)}, bf16[1024,768]{1,0:T(8,128)(2,1)}) fusion(bf16[1024,1536]{1,0:T(8,128)(2,1)} %all-gather.6.cloned.1.call-done), kind=kLoop, calls=%fused_computation.110 | loop fusion | bytes 6291456 | tf_op jit(solution)/shard_map/slice | solution.py:126
  259.2 2.6 copy.82
  261.9 2.6 copy.85
  264.5 2.6 multiply_reduce_fusion
  267.1 2.7 copy-done.1
  269.8 1.9 fusion.1
  271.7 52.7 %all-gather.8.cloned.1.call-done = bf16[1024,1536]{1,0:T(8,128)(2,1)} async-done(((bf16[8,1536]{1,0:T(8,128)(2,1)}), bf16[1024,1536]{1,0:T(8,128)(2,1)}) %all-gather.8.cloned.1.call-update) | async-done | bytes 3145744 | tf_op jit(solution)/shard_map/all_gather | solution.py:143
  324.3 3.8 %fusion.67 = (bf16[1024,768]{1,0:T(8,128)(2,1)}, bf16[1024,768]{1,0:T(8,128)(2,1)}) fusion(bf16[1024,1536]{1,0:T(8,128)(2,1)} %all-gather.8.cloned.1.call-done), kind=kLoop, calls=%fused_computation.109 | loop fusion | bytes 6291456 | tf_op jit(solution)/shard_map/slice | solution.py:146
  328.1 2.6 copy.83
  330.7 1.8 fusion.69
  332.5 0.7 copy-done.6
  334.1 0.7 sub.77
  334.8 1.5 sub.78
  336.2 2.6 copy.86
  338.8 2.1 fusion.15
  340.9 1.0 broadcast_in_dim.128
  341.9 2.1 copy.89
  344.0 0.7 broadcast_subtract_fusion
  344.8 4.8 %fusion.26 = bf16[128,12,64]{0,2,1:T(8,128)(2,1)S(1)} fusion(bf16[1024,12,64]{0,2,1:T(8,128)(2,1)} %bitcast.74, f32[12,128,1024]{2,1,0:T(8,128)} %copy-done.1, f32[12,128]{1,0:T(8,128)S(1)} %get-tuple-element.23, f32[128,12,64]{0,2,1:T(8,128)} %copy.89, f32[128,12]{0,1:T(8,128)S(1)} %get-tuple-element.8, f32[128,12]{0,1:T(8,128)} %bitcast.79, ...), kind=kOutput, calls=%fused_computation.33 | convolution fusion | flops 206635008 | bytes 8480256 | tf_op jit(solution)/shard_map/hqk,khd->qhd/dot_general | solution.py:37
  349.6 1.0 fusion.14
  (45 shorter events, 2.0 us)
Async XLA Ops:
  6.5 222.0 %copy-start = (bf16[768,2304]{1,0:T(8,128)(2,1)S(1)}, bf16[768,2304]{1,0:T(8,128)(2,1)}, u32[]{:S(2)}) copy-start(bf16[768,2304]{1,0:T(8,128)(2,1)} %param.25) | copy-start | bytes 10616836
  6.5 69.4 %all-gather.4.cloned.1.call-start = ((), (), s32[]{:S(2)}) async-start(), calls=%async_computation.3 | async-start | bytes 6684672 | tf_op jit(solution)/shard_map/all_gather | solution.py:64
  11.1 181.2 %reduce-scatter.2.cloned.1.call-start = ((), (), s32[]{:S(2)}) async-start(), calls=%async_computation.4 | async-start | bytes 13369344 | tf_op jit(solution)/shard_map/reduce_scatter | solution.py:68
  96.6 95.8 %copy-start.9 = (f32[1536]{0:T(1024)S(1)}, f32[1536]{0:T(1024)}, u32[]{:S(2)}) copy-start(f32[1536]{0:T(1024)} %param.19) | copy-start | bytes 18436
  96.6 98.8 %copy-start.11 = (f32[1536]{0:T(1024)S(1)}, f32[1536]{0:T(1024)}, u32[]{:S(2)}) copy-start(f32[1536]{0:T(1024)} %param.20) | copy-start | bytes 18436
  103.8 18.1 %all-to-all-start = ((s32[128,2,3]{2,1,0:T(2,128)}), s32[128,2,3]{2,1,0:T(2,128)}, u32[]{:S(2)}, u32[]{:S(2)}) async-start(s32[128,2,3]{2,1,0:T(2,128)} %bitcast.76), calls=%async_computation | async-start | bytes 262144 | tf_op jit(solution)/shard_map/all_to_all | solution.py:98
  192.4 3.0 copy-start.2
  192.4 3.0 copy-start.3
  200.6 28.0 %copy-start.12 = (f32[768]{0:T(1024)S(1)}, f32[768]{0:T(1024)}, u32[]{:S(2)}) copy-start(f32[768]{0:T(1024)} %param.24) | copy-start | bytes 9220
  202.5 19.8 %all-to-all-start.1 = ((bf16[128,2,768]{2,1,0:T(2,128)(2,1)}), bf16[128,2,768]{2,1,0:T(2,128)(2,1)}, u32[]{:S(2)}, u32[]{:S(2)}) async-start(bf16[128,2,768]{2,1,0:T(2,128)(2,1)} %reshape.194), calls=%async_computation.2 | async-start | bytes 786432 | tf_op jit(solution)/shard_map/all_to_all | solution.py:91
  210.3 45.2 %all-gather.6.cloned.1.call-start = ((), (), s32[]{:S(2)}) async-start(), calls=%async_computation.5 | async-start | bytes 3538944 | tf_op jit(solution)/shard_map/all_gather | solution.py:123
  228.3 0.9 copy-start.4
  228.5 2.4 copy-start.13
  229.2 0.8 copy-start.7
  230.9 93.4 %all-gather.8.cloned.1.call-start = ((), (), s32[]{:S(2)}) async-start(), calls=%async_computation.6 | async-start | bytes 3170304 | tf_op jit(solution)/shard_map/all_gather | solution.py:143
  267.1 2.7 copy-start.1
  332.5 0.7 copy-start.6
  333.5 0.6 copy-start.10
  344.8 4.8 %copy-start.5 = (f32[128,768]{1,0:T(8,128)S(1)}, f32[128,768]{1,0:T(8,128)}, u32[]{:S(2)}) copy-start(f32[128,768]{1,0:T(8,128)} %copy-done.4) | copy-start | bytes 1179652
  344.8 4.8 %copy-start.8 = (bf16[768,768]{1,0:T(8,128)(2,1)S(1)}, bf16[768,768]{1,0:T(8,128)(2,1)}, u32[]{:S(2)}) copy-start(bf16[768,768]{1,0:T(8,128)(2,1)} %param.27) | copy-start | bytes 3538948
Sparse Core Ops, SparseCore 0:
  11.3 64.6 all-gather.3
  96.7 95.5 reduce-scatter.1
  231.0 24.3 all-gather.5
  258.4 65.8 all-gather.7
where the time goes:
time: 358 us; the launch traced here: 357 us
  waiting for transfers between devices  210 us (59%)
  local copies, waits for them, and re-layouts  56.9 us (16%)
  matrix products  36.7 us (10%)
  other arithmetic  24.2 us (7%)
  starting transfers between devices  16.2 us (5%)
  between operations  13.4 us (4%)
    reduce_scatter x1, waiting for transfers between devices, body(): lax.psum_scatter(jnp.dot(hidden, w_down, preferred_element_type=jnp.float...  68.9 us
    all_gather x1, waiting for transfers between devices, body(): shard_rows = lax.all_gather(normed, 'tile', axis=0, tiled=True)  64.7 us
    all_gather x1, waiting for transfers between devices, body(): lax.all_gather(select(keys_values, 2), ('tile', 'seq'), axis=0, tiled=True)  52.7 us
    dot_general x1, matrix products, body(): jnp.dot(hidden, w_down, preferred_element_type=jnp.float32)  14.6 us
    all_to_all x1, waiting for transfers between devices, body(): lax.all_to_all(meta_table.reshape(devices, capacity, 3), ('tile', 'seq'),...  9.2 us
    all_gather x1, waiting for transfers between devices, body(): segment_kv = lax.all_gather(keys_values, 'seq', axis=0, tiled=True)  8.69 us
    all_to_all x1, starting transfers between devices, body(): lax.all_to_all(meta_table.reshape(devices, capacity, 3), ('tile', 'seq'),...  8.32 us
    all_to_all x1, starting transfers between devices, body(): lax.all_to_all(payload.reshape(devices, capacity, hidden_width), ('tile',...  7.79 us
  transfers between devices with their start and end apart: 6, of which 6 were waited for; matrix products, arithmetic and copies ran while one was open for 13% of the time, Pallas kernels for 0%

commit v1 on v0

--- a/solution.py
+++ b/solution.py
@@ -6,6 +6,19 @@
 HEAD_COUNT = 12
 HEAD_WIDTH = 64
 SEGMENT_SPACING = 16
+
+
+def collect(shard, axis, dim):
+    size, place, width = (lax.axis_size(axis), lax.axis_index(axis), shard.shape[dim])
+    upward = [(i, (i + 1) % size) for i in range(size)]
+    filled = jnp.zeros((*shard.shape[:dim], size * width, *shard.shape[dim + 1 :]), shard.dtype)
+    carried = shard
+    for hop in range(size):
+        source = (place - hop) % size
+        filled = lax.dynamic_update_slice_in_dim(filled, carried, source * width, axis=dim)
+        if hop < size - 1:
+            carried = lax.ppermute(carried, axis, upward)
+    return filled
 
 
 def layer_norm(sender_rows, gain):
@@ -120,7 +133,7 @@
     qkv = jnp.dot(normed_seq, w_qkv, preferred_element_type=jnp.float32).astype(jnp.bfloat16)
     queries = qkv[:, :hidden_width]
     keys_values = qkv[:, hidden_width:]
-    segment_kv = lax.all_gather(keys_values, "seq", axis=0, tiled=True)
+    segment_kv = collect(keys_values, "seq", 0)
     near_out, nearby_logsumexp = attend(
         queries.reshape(resident_rows, HEAD_COUNT, HEAD_WIDTH),
         segment_kv[:, :hidden_width].reshape(-1, HEAD_COUNT, HEAD_WIDTH),

time: 358 us -> 328 us (0.916)
  the two profiles are of different devices: /device:TPU:1 before, /device:TPU:0 now
where the time goes in v1:
time: 328 us; the launch traced here: 327 us
  waiting for transfers between devices  201 us (61%)
  local copies, waits for them, and re-layouts  44 us (13%)
  matrix products  34.1 us (10%)
  other arithmetic  17.4 us (5%)
  starting transfers between devices  17 us (5%)
  between operations  13.5 us (4%)
    reduce_scatter x1, waiting for transfers between devices, body(): lax.psum_scatter(jnp.dot(hidden, w_down, preferred_element_type=jnp.float...  73.1 us
    all_gather x1, waiting for transfers between devices, body(): shard_rows = lax.all_gather(normed, 'tile', axis=0, tiled=True)  64 us
    ppermute x7, waiting for transfers between devices, collect(): carried = lax.ppermute(carried, axis, upward)  50.4 us
    dot_general x1, matrix products, body(): jnp.dot(hidden, w_down, preferred_element_type=jnp.float32)  14.7 us
    all_to_all x1, starting transfers between devices, body(): lax.all_to_all(meta_table.reshape(devices, capacity, 3), ('tile', 'seq'),...  8.79 us
    ppermute x7, local copies, waits for them, and re-layouts, collect(): carried = lax.ppermute(carried, axis, upward)  8.51 us
    all_to_all x1, waiting for transfers between devices, body(): lax.all_to_all(meta_table.reshape(devices, capacity, 3), ('tile', 'seq'),...  8.07 us
    all_to_all x1, starting transfers between devices, body(): lax.all_to_all(payload.reshape(devices, capacity, hidden_width), ('tile',...  8.05 us
  transfers between devices with their start and end apart: 12, of which 11 were waited for; matrix products, arithmetic and copies ran while one was open for 9% of the time, Pallas kernels for 0%

profile of v1, /device:TPU:0, one launch (start us, length us, event | category | flops | bytes accessed | tf_op | source)
XLA Modules:
  0.0 327.1 jit_solution(11525024215987923628)
XLA Ops:
  6.5 1.3 convert_reduce_fusion
  7.8 1.2 fusion.31
  9.1 2.0 fusion.33
  11.2 64.0 %all-gather.3.cloned.1.call-done = bf16[2048,1536]{1,0:T(8,128)(2,1)} async-done(((bf16[128,1536]{1,0:T(8,128)(2,1)}), bf16[2048,1536]{1,0:T(8,128)(2,1)}) %all-gather.3.cloned.1.call-update) | async-done | bytes 6291472 | tf_op jit(solution)/shard_map/all_gather | solution.py:77
  75.2 6.0 %fusion.70 = f32[2048,256]{1,0:T(8,128)} fusion(bf16[2048,1536]{1,0:T(8,128)(2,1)} %all-gather.3.cloned.1.call-done, bf16[1536,256]{1,0:T(8,128)(2,1)} %param.16), kind=kOutput, calls=%fused_computation.120 | convolution fusion | flops 1610612736 | bytes 9175040 | tf_op jit(solution)/shard_map/dot_general | solution.py:78
  81.2 14.7 %fusion.7 = f32[2048,1536]{1,0:T(8,128)} fusion(bf16[256,1536]{1,0:T(8,128)(2,1)} %param.18, bf16[2048,1536]{1,0:T(8,128)(2,1)} %all-gather.3.cloned.1.call-done, bf16[1536,256]{1,0:T(8,128)(2,1)} %param.17, f32[2048,256]{1,0:T(8,128)} %fusion.70), kind=kOutput, calls=%fused_computation.14 | convolution fusion | flops 3224371200 | bytes 22544384 | tf_op jit(solution)/shard_map/dot_general | solution.py:82
  95.9 0.6 copy-done.16
  96.6 0.7 copy.105
  97.5 1.8 scatter_custom_fusion
  99.3 8.8 %all-to-all-start = ((s32[128,2,3]{2,1,0:T(2,128)}), s32[128,2,3]{2,1,0:T(2,128)}, u32[]{:S(2)}, u32[]{:S(2)}) async-start(s32[128,2,3]{2,1,0:T(2,128)} %bitcast.76), calls=%async_computation | async-start | bytes 262144 | tf_op jit(solution)/shard_map/all_to_all | solution.py:111
  108.1 0.7 iota_compare_fusion.1
  108.8 0.6 negate_power_fusion
  109.4 8.1 %all-to-all-done = s32[128,2,3]{2,1,0:T(2,128)} async-done(((s32[128,2,3]{2,1,0:T(2,128)}), s32[128,2,3]{2,1,0:T(2,128)}, u32[]{:S(2)}, u32[]{:S(2)}) %all-to-all-start) | async-done | bytes 3104 | tf_op jit(solution)/shard_map/all_to_all | solution.py:111
  117.4 1.0 copy.129
  118.4 73.1 %reduce-scatter.2.cloned.1.call-done = f32[128,1536]{1,0:T(8,128)} async-done(((f32[2048,1536]{1,0:T(8,128)}), f32[128,1536]{1,0:T(8,128)}) %reduce-scatter.2.cloned.1.call-update) | async-done | bytes 786448 | tf_op jit(solution)/shard_map/reduce_scatter | solution.py:81
  191.6 1.4 fusion.39
  193.0 1.5 multiply_reduce_fusion.1
  194.5 3.3 %convolution_convert_fusion.1 = bf16[128,768]{1,0:T(8,128)(2,1)} fusion(bf16[1536,768]{1,0:T(8,128)(2,1)} %param.21, f32[1536]{0:T(1024)} %param.20, f32[128]{0:T(128)S(1)} %add_rsqrt_fusion.1, f32[128]{0:T(128)S(1)} %broadcast_multiply_fusion.1, bf16[128,1536]{1,0:T(8,128)(2,1)} %param.14, f32[128,1536]{1,0:T(8,128)} %reduce-scatter.2.cloned.1.call-done, ...), kind=kOutput, calls=%fused_computation.25 | convolution fusion | flops 303464448 | bytes 3748864 | tf_op jit(solution)/shard_map/dot_general | solution.py:89
  197.8 2.3 scatter_custom_fusion.1
  200.0 1.9 reshape.194
  201.9 8.0 %all-to-all-start.1 = ((bf16[128,2,768]{2,1,0:T(2,128)(2,1)}), bf16[128,2,768]{2,1,0:T(2,128)(2,1)}, u32[]{:S(2)}, u32[]{:S(2)}) async-start(bf16[128,2,768]{2,1,0:T(2,128)(2,1)} %reshape.194), calls=%async_computation.2 | async-start | bytes 786432 | tf_op jit(solution)/shard_map/all_to_all | solution.py:104
  210.6 2.2 scatter_custom_fusion.3
  212.8 1.1 fusion.52
  213.9 2.5 multiply_sine_fusion.1
  216.3 5.4 %all-to-all-done.1 = bf16[128,2,768]{2,1,0:T(2,128)(2,1)} async-done(((bf16[128,2,768]{2,1,0:T(2,128)(2,1)}), bf16[128,2,768]{2,1,0:T(2,128)(2,1)}, u32[]{:S(2)}, u32[]{:S(2)}) %all-to-all-start.1) | async-done | bytes 393248 | tf_op jit(solution)/shard_map/all_to_all | solution.py:104
  221.7 1.9 reshape.224
  223.6 2.7 scatter_custom_fusion.2
  226.3 1.4 fusion.66
  228.5 0.7 convolution_convert_fusion
  229.2 0.8 copy-done.5
  230.0 0.9 reshape.199
  231.3 0.7 reshape.200
  232.1 8.4 %collective-permute-done = bf16[128,1536]{1,0:T(8,128)(2,1)S(1)} collective-permute-done((bf16[128,1536]{1,0:T(8,128)(2,1)S(1)}, bf16[128,1536]{1,0:T(8,128)(2,1)S(1)}, u32[]{:S(2)}, u32[]{:S(2)}) %collective-permute-start) | collective-permute-done | bytes 393248 | tf_op jit(solution)/shard_map/ppermute | solution.py:20
  240.5 8.5 %collective-permute-done.1 = bf16[128,1536]{1,0:T(8,128)(2,1)S(1)} collective-permute-done((bf16[128,1536]{1,0:T(8,128)(2,1)S(1)}, bf16[128,1536]{1,0:T(8,128)(2,1)S(1)}, u32[]{:S(2)}, u32[]{:S(2)}) %collective-permute-start.1) | collective-permute-done | bytes 393248 | tf_op jit(solution)/shard_map/ppermute | solution.py:20
  249.0 8.5 %collective-permute-done.2 = bf16[128,1536]{1,0:T(8,128)(2,1)} collective-permute-done((bf16[128,1536]{1,0:T(8,128)(2,1)S(1)}, bf16[128,1536]{1,0:T(8,128)(2,1)}, u32[]{:S(2)}, u32[]{:S(2)}) %collective-permute-start.2) | collective-permute-done | bytes 393248 | tf_op jit(solution)/shard_map/ppermute | solution.py:20
  257.6 0.7 broadcast_in_dim.122
  258.6 0.9 slice.53
  259.5 0.8 copy.111
  260.7 0.8 select_reduce_fusion.1
  262.0 1.2 copy.113
  263.2 3.4 %collective-permute-done.3 = bf16[128,1536]{1,0:T(8,128)(2,1)} collective-permute-done((bf16[128,1536]{1,0:T(8,128)(2,1)}, bf16[128,1536]{1,0:T(8,128)(2,1)}, u32[]{:S(2)}, u32[]{:S(2)}) %collective-permute-start.3) | collective-permute-done | bytes 393248 | tf_op jit(solution)/shard_map/ppermute | solution.py:20
  266.7 1.2 copy.114
  268.1 1.2 copy.115
  269.3 6.2 %collective-permute-done.4 = bf16[128,1536]{1,0:T(8,128)(2,1)} collective-permute-done((bf16[128,1536]{1,0:T(8,128)(2,1)}, bf16[128,1536]{1,0:T(8,128)(2,1)}, u32[]{:S(2)}, u32[]{:S(2)}) %collective-permute-start.4) | collective-permute-done | bytes 393248 | tf_op jit(solution)/shard_map/ppermute | solution.py:20
  275.6 1.2 copy.116
  277.0 1.2 copy.117
  278.2 7.6 %collective-permute-done.5 = bf16[128,1536]{1,0:T(8,128)(2,1)} collective-permute-done((bf16[128,1536]{1,0:T(8,128)(2,1)}, bf16[128,1536]{1,0:T(8,128)(2,1)}, u32[]{:S(2)}, u32[]{:S(2)}) %collective-permute-start.5) | collective-permute-done | bytes 393248 | tf_op jit(solution)/shard_map/ppermute | solution.py:20
  286.0 1.2 copy.118
  287.3 7.9 %collective-permute-done.6 = bf16[128,1536]{1,0:T(8,128)(2,1)} collective-permute-done((bf16[128,1536]{1,0:T(8,128)(2,1)}, bf16[128,1536]{1,0:T(8,128)(2,1)}, u32[]{:S(2)}, u32[]{:S(2)}) %collective-permute-start.6) | collective-permute-done | bytes 393248 | tf_op jit(solution)/shard_map/ppermute | solution.py:20
  295.2 1.2 copy.119
  296.6 1.5 fusion.68
  298.1 1.1 multiply_reduce_fusion
  299.2 2.7 copy-done.2
  301.9 1.9 fusion.1
  303.8 3.2 fusion.67
  307.0 1.7 copy.120
  308.7 1.2 fusion.69
  310.1 0.6 copy-done.11
  310.7 0.7 sub.106
  311.4 0.7 copy.122
  312.2 1.3 fusion.15
  313.6 1.0 copy.125
  314.6 4.8 %fusion.26 = bf16[128,12,64]{0,2,1:T(8,128)(2,1)S(1)} fusion(bf16[1024,12,64]{0,2,1:T(8,128)(2,1)} %bitcast.74, f32[12,128,1024]{2,1,0:T(8,128)} %copy-done.2, f32[12,128]{1,0:T(8,128)S(1)} %get-tuple-element.23, f32[128,12,64]{0,2,1:T(8,128)} %copy.125, f32[128,12]{0,1:T(8,128)S(1)} %get-tuple-element.8, f32[128,12]{0,1:T(8,128)} %bitcast.79, ...), kind=kOutput, calls=%fused_computation.33 | convolution fusion | flops 206635008 | bytes 8480256 | tf_op jit(solution)/shard_map/hqk,khd->qhd/dot_general | solution.py:50
  319.5 1.0 fusion.14
  (83 shorter events, 4.7 us)
Async XLA Ops:
  6.5 222.0 %copy-start = (bf16[768,2304]{1,0:T(8,128)(2,1)S(1)}, bf16[768,2304]{1,0:T(8,128)(2,1)}, u32[]{:S(2)}) copy-start(bf16[768,2304]{1,0:T(8,128)(2,1)} %param.25) | copy-start | bytes 10616836
  6.5 68.6 %all-gather.3.cloned.1.call-start = ((), (), s32[]{:S(2)}) async-start(), calls=%async_computation.3 | async-start | bytes 6684672 | tf_op jit(solution)/shard_map/all_gather | solution.py:77
  11.1 180.4 %reduce-scatter.2.cloned.1.call-start = ((), (), s32[]{:S(2)}) async-start(), calls=%async_computation.4 | async-start | bytes 13369344 | tf_op jit(solution)/shard_map/reduce_scatter | solution.py:81
  95.9 0.7 copy-start.16
  95.9 0.7 copy-start.18
  95.9 95.7 %copy-start.10 = (f32[1536]{0:T(1024)S(1)}, f32[1536]{0:T(1024)}, u32[]{:S(2)}) copy-start(f32[1536]{0:T(1024)} %param.19) | copy-start | bytes 18436
  97.5 1.8 copy-start.19
  99.3 18.1 %all-to-all-start = ((s32[128,2,3]{2,1,0:T(2,128)}), s32[128,2,3]{2,1,0:T(2,128)}, u32[]{:S(2)}, u32[]{:S(2)}) async-start(s32[128,2,3]{2,1,0:T(2,128)} %bitcast.76), calls=%async_computation | async-start | bytes 262144 | tf_op jit(solution)/shard_map/all_to_all | solution.py:111
  197.8 30.8 %copy-start.15 = (f32[768]{0:T(1024)S(1)}, f32[768]{0:T(1024)}, u32[]{:S(2)}) copy-start(f32[768]{0:T(1024)} %param.24) | copy-start | bytes 9220
  201.9 19.8 %all-to-all-start.1 = ((bf16[128,2,768]{2,1,0:T(2,128)(2,1)}), bf16[128,2,768]{2,1,0:T(2,128)(2,1)}, u32[]{:S(2)}, u32[]{:S(2)}) async-start(bf16[128,2,768]{2,1,0:T(2,128)(2,1)} %reshape.194), calls=%async_computation.2 | async-start | bytes 786432 | tf_op jit(solution)/shard_map/all_to_all | solution.py:104
  210.0 93.8 %all-gather.5.cloned.1.call-start = ((), (), s32[]{:S(2)}) async-start(), calls=%async_computation.5 | async-start | bytes 3170304 | tf_op jit(solution)/shard_map/all_gather | solution.py:156
  210.0 0.5 copy-start.17
  227.7 0.8 copy-start.3
  229.2 0.8 copy-start.5
  232.1 8.4 %collective-permute-start = (bf16[128,1536]{1,0:T(8,128)(2,1)S(1)}, bf16[128,1536]{1,0:T(8,128)(2,1)S(1)}, u32[]{:S(2)}, u32[]{:S(2)}) collective-permute-start(bf16[128,1536]{1,0:T(8,128)(2,1)S(1)} %slice.54), channel_id=1, source_target_pairs={{0,1},{1,2},{2,3},{3,4},{4,5},{5,6},{6,7},{7,0},{8,9},{9,10},{10,1... | collective-permute-start | bytes 1179656 | tf_op jit(solution)/shard_map/ppermute | solution.py:20
  240.5 17.8 %copy-start.9 = (bf16[128,1536]{1,0:T(8,128)(2,1)}, bf16[128,1536]{1,0:T(8,128)(2,1)S(1)}, u32[]{:S(2)}) copy-start(bf16[128,1536]{1,0:T(8,128)(2,1)S(1)} %collective-permute-done) | copy-start | bytes 1179652
  240.5 8.5 %collective-permute-start.1 = (bf16[128,1536]{1,0:T(8,128)(2,1)S(1)}, bf16[128,1536]{1,0:T(8,128)(2,1)S(1)}, u32[]{:S(2)}, u32[]{:S(2)}) collective-permute-start(bf16[128,1536]{1,0:T(8,128)(2,1)S(1)} %collective-permute-done), channel_id=1, source_target_pairs={{0,1},{1,2},{2,3},{3,4},{4,5},{5,6},{6,7},{7,0},{8,9},{9,10},{10,1... | collective-permute-start | bytes 1179656 | tf_op jit(solution)/shard_map/ppermute | solution.py:20
  249.0 10.5 %copy-start.8 = (bf16[128,1536]{1,0:T(8,128)(2,1)}, bf16[128,1536]{1,0:T(8,128)(2,1)S(1)}, u32[]{:S(2)}) copy-start(bf16[128,1536]{1,0:T(8,128)(2,1)S(1)} %collective-permute-done.1) | copy-start | bytes 1179652
  249.0 8.5 %collective-permute-start.2 = (bf16[128,1536]{1,0:T(8,128)(2,1)S(1)}, bf16[128,1536]{1,0:T(8,128)(2,1)}, u32[]{:S(2)}, u32[]{:S(2)}) collective-permute-start(bf16[128,1536]{1,0:T(8,128)(2,1)S(1)} %collective-permute-done.1), channel_id=1, source_target_pairs={{0,1},{1,2},{2,3},{3,4},{4,5},{5,6},{6,7},{7,0},{8,9},{9,10},{10,1... | collective-permute-start | bytes 1179656 | tf_op jit(solution)/shard_map/ppermute | solution.py:20
  257.5 9.1 %collective-permute-start.3 = (bf16[128,1536]{1,0:T(8,128)(2,1)}, bf16[128,1536]{1,0:T(8,128)(2,1)}, u32[]{:S(2)}, u32[]{:S(2)}) collective-permute-start(bf16[128,1536]{1,0:T(8,128)(2,1)} %collective-permute-done.2), channel_id=1, source_target_pairs={{0,1},{1,2},{2,3},{3,4},{4,5},{5,6},{6,7},{7,0},{8,9},{9,10},{10,1... | collective-permute-start | bytes 1179656 | tf_op jit(solution)/shard_map/ppermute | solution.py:20
  266.6 8.9 %collective-permute-start.4 = (bf16[128,1536]{1,0:T(8,128)(2,1)}, bf16[128,1536]{1,0:T(8,128)(2,1)}, u32[]{:S(2)}, u32[]{:S(2)}) collective-permute-start(bf16[128,1536]{1,0:T(8,128)(2,1)} %collective-permute-done.3), channel_id=1, source_target_pairs={{0,1},{1,2},{2,3},{3,4},{4,5},{5,6},{6,7},{7,0},{8,9},{9,10},{10,1... | collective-permute-start | bytes 1179656 | tf_op jit(solution)/shard_map/ppermute | solution.py:20
  275.5 10.3 %collective-permute-start.5 = (bf16[128,1536]{1,0:T(8,128)(2,1)}, bf16[128,1536]{1,0:T(8,128)(2,1)}, u32[]{:S(2)}, u32[]{:S(2)}) collective-permute-start(bf16[128,1536]{1,0:T(8,128)(2,1)} %collective-permute-done.4), channel_id=1, source_target_pairs={{0,1},{1,2},{2,3},{3,4},{4,5},{5,6},{6,7},{7,0},{8,9},{9,10},{10,1... | collective-permute-start | bytes 1179656 | tf_op jit(solution)/shard_map/ppermute | solution.py:20
  285.8 9.4 %collective-permute-start.6 = (bf16[128,1536]{1,0:T(8,128)(2,1)}, bf16[128,1536]{1,0:T(8,128)(2,1)}, u32[]{:S(2)}, u32[]{:S(2)}) collective-permute-start(bf16[128,1536]{1,0:T(8,128)(2,1)} %collective-permute-done.5), channel_id=1, source_target_pairs={{0,1},{1,2},{2,3},{3,4},{4,5},{5,6},{6,7},{7,0},{8,9},{9,10},{10,1... | collective-permute-start | bytes 1179656 | tf_op jit(solution)/shard_map/ppermute | solution.py:20
  296.6 1.5 copy-start.7
  299.2 2.7 copy-start.2
  310.1 0.6 copy-start.11
  312.2 2.4 copy-start.12
  312.2 2.4 copy-start.13
  312.2 2.4 copy-start.14
  314.6 4.9 %copy-start.4 = (f32[128,768]{1,0:T(8,128)S(1)}, f32[128,768]{1,0:T(8,128)}, u32[]{:S(2)}) copy-start(f32[128,768]{1,0:T(8,128)} %copy-done.3) | copy-start | bytes 1179652
  314.6 4.9 %copy-start.6 = (bf16[768,768]{1,0:T(8,128)(2,1)S(1)}, bf16[768,768]{1,0:T(8,128)(2,1)}, u32[]{:S(2)}) copy-start(bf16[768,768]{1,0:T(8,128)(2,1)} %param.27) | copy-start | bytes 3538948
  314.6 5.9 %copy-start.1 = (bf16[768,2304]{1,0:T(8,128)(2,1)S(1)}, bf16[768,2304]{1,0:T(8,128)(2,1)}, u32[]{:S(2)}) copy-start(bf16[768,2304]{1,0:T(8,128)(2,1)} %param.25) | copy-start | bytes 10616836
Sparse Core Ops, SparseCore 0:
  11.3 63.8 all-gather.2
  96.0 95.4 reduce-scatter.1
  232.2 62.1 all-gather.4
